TPU v7x, 128 devices: a whole 4x4x4 slice. The times are simulated.
128 devices in a mesh: dp: 2 (over core), pipe: 4 (over x), height: 16 (over z, y).
Axes of the slice: x: 4, y: 4, z: 4, core: 2. Of those that a mesh axis runs over, the one named last changes fastest.
Arguments:
- video: bfloat16 [2, 12, 64, 16, 256], P('dp', None, 'height'), may hold values from -48 to 48
- kernels: bfloat16 [4, 6912, 256], P('pipe'), may hold values from -0.078125 to 0.078125
- gains: float32 [4, 256], P('pipe'), may hold values from 0.1 to 1.9
- shifts: float32 [4, 256], P('pipe'), may hold values from -3 to 3
- out_grad: bfloat16 [2, 12, 64, 16, 256], P('dp', None, 'height'), may hold values from -0.48 to 0.48
Outputs:
- kernel_grad: float32 [4, 6912, 256], P('pipe', ('dp', 'height'))
- norm_grad: float32 [4, 2, 256], P('pipe')
All inputs are finite; a program needn't handle non-finite values.
Results may differ from a plain program's by a relative error of at most 0.0067.
Values may be sent and summed in bfloat16 or wider, within the bound.
A program may use at most 64 MiB of HBM per device.

v0:
```python
import functools

import jax
import jax.numpy as jnp
from jax import lax
from jax.experimental import pallas as pl
from jax.experimental.pallas import tpu as pltpu
from jax.sharding import PartitionSpec as P

GROUPS = 32
F = 4
SPANS = 3
NB = 16
LAYERS = 4
R = 4
W16 = 16
C = 256
POS = F * R * W16
GSIZE = float(POS * NB * (C // GROUPS))
HALF = 3456
SHARE = 216
EPS = 1e-05
f32 = jnp.float32
bf16 = jnp.bfloat16
MESH = pl.DeviceIdType.MESH


def group_mate(x, d):
    lane = lax.broadcasted_iota(jnp.int32, x.shape, 1)
    return jnp.where((lane & d) != 0, pltpu.roll(x, d, 1), pltpu.roll(x, C - d, 1))


def group_sum(x):
    for d in (1, 2, 4):
        x = x + group_mate(x, d)
    return x


def even(x):
    return (lax.broadcasted_iota(jnp.int32, x.shape, 1) & 1) == 0


def spread(x):
    return jnp.where(even(x), x, pltpu.roll(x, 1, 1))


def summary(mean_c, dev_c):
    both = jnp.concatenate([mean_c, dev_c], axis=0)
    count = float(POS)
    for d in (1, 2, 4):
        mate = group_mate(both, d)
        gap = both[0:1] - mate[0:1]
        both = jnp.concatenate(
            [0.5 * (both[0:1] + mate[0:1]), both[1:2] + mate[1:2] + (0.5 * count) * gap * gap], axis=0
        )
        count = 2.0 * count
    return both[0:1], jnp.where(even(mean_c), both[0:1], both[1:2])


def gradient_summary(gpre, normed, gain):
    sums = jnp.concatenate(
        [jnp.sum(gpre * normed, axis=0, keepdims=True), jnp.sum(gpre, axis=0, keepdims=True)], axis=0
    )
    sums = group_sum(sums * gain)
    return jnp.where(even(gain), sums[0:1], sums[1:2])


def combine(table):
    sums = jnp.sum(table, axis=0)
    mean = sums * (1.0 / NB)
    between = jnp.sum((table - mean[None]) ** 2, axis=0)
    dev = pltpu.roll(sums, C - 1, 1) + (GSIZE / NB) * between
    both = spread(jnp.concatenate([mean, lax.rsqrt(dev * (1.0 / GSIZE) + EPS)], axis=0))
    return both[0:1], both[1:2]


def sigmoid(v):
    return 0.5 * jnp.tanh(0.5 * v) + 0.5


def put_shifted(dst, frame, x):
    n = x.shape[1]
    v = x.reshape(F * n, W16, C)
    col = lax.broadcasted_iota(jnp.int32, v.shape, 1)
    left = jnp.where(col == 0, 0.0, pltpu.roll(v, 1, 1))
    right = jnp.where(col == W16 - 1, 0.0, pltpu.roll(v, W16 - 1, 1))
    for c, part in enumerate((left, v, right)):
        dst[pl.ds(frame, F), :, :, C * c : C * c + C] = part.astype(bf16).reshape(F, n, W16, C)


def kernel(
    video, kern, gains, shifts, ograd, out_k, out_n,
    W, XP, XR, XN, RL, CP, CO, CF, SS, PX, G, GG, UR, UO, STP, STO, SB, SBO, GO, GP, NP, LP, NO, LO, MI,
    WG, A1S, A1R, B1S, B1R, A2S, A2R, B2S, B2R, NG, NT,
    ready, w_sem, xpc, xph, rl, cp, stp, sto, cfh, ur, sb, px, pg, a1, b1, a2, b2, ngs, gps, nt,
    s_x, s_xn, s_xr, s_rl, s_c, s_ch, s_sto, s_stn, s_px, s_pg, s_ur, s_og, s_sb, s_sbo, s_a1, s_b1, s_a2, s_b2, s_ng, s_gp, s_nt,
):
    dp, s, h = lax.axis_index("dp"), lax.axis_index("pipe"), lax.axis_index("height")
    nxt, prv = lax.rem(s + 1, LAYERS), lax.rem(s + LAYERS - 1, LAYERS)
    up, dn = lax.rem(h + NB - 1, NB), lax.rem(h + 1, NB)
    other = 1 - dp
    zz, yy = lax.div(h, 4), lax.rem(h, 4)
    steps = [(i, j) for i in range(4) for j in range(4)]
    steps.sort(key=lambda o: -(min(o[0], 4 - o[0]) + min(o[1], 4 - o[1])))
    bands = [lax.rem(zz + i, 4) * 4 + lax.rem(yy + j, 4) for i, j in steps]

    def remote(src, dst, ssem, rsem, dev):
        pltpu.make_async_remote_copy(
            src_ref=src, dst_ref=dst, send_sem=ssem, recv_sem=rsem, device_id=dev, device_id_type=MESH
        ).start()

    def await_bytes(ref, sem):
        pltpu.make_async_copy(ref, ref, sem).wait()

    inside = (h > 0) & (h < NB - 1)

    def await_edges(ref, k, sem, rows=0):
        @pl.when(inside)
        def _():
            await_bytes(ref.at[fr(k), pl.ds(0, rows + 2)], sem)

        @pl.when(jnp.logical_not(inside))
        def _():
            await_bytes(ref.at[fr(k), pl.ds(0, rows + 1)], sem)

    def send_edges(src, first, last, dst, k, ssem, rsem, layer):
        @pl.when(h > 0)
        def _():
            remote(src.at[fr(k), pl.ds(first, 1)], dst.at[fr(k), pl.ds(5, 1)], ssem, rsem, (dp, layer, up))

        @pl.when(h < NB - 1)
        def _():
            remote(src.at[fr(k), pl.ds(last, 1)], dst.at[fr(k), pl.ds(0, 1)], ssem, rsem, (dp, layer, dn))

    def fr(k, first=0):
        return pl.ds(F * k + first, F)

    wcopy = pltpu.make_async_copy(kern.at[0], W, w_sem)
    wcopy.start()
    barrier = pltpu.get_barrier_semaphore()
    far = lax.rem(s + 2, LAYERS)

    @pl.when(s == LAYERS - 1)
    def _():
        @pl.when(h > 0)
        def _():
            pl.semaphore_signal(barrier, inc=1, device_id=(dp, far, up), device_id_type=MESH)

        @pl.when(h < NB - 1)
        def _():
            pl.semaphore_signal(barrier, inc=1, device_id=(dp, far, dn), device_id_type=MESH)

        pl.semaphore_signal(barrier, inc=1, device_id=(dp, far, h), device_id_type=MESH)

    for b in bands[:-1]:
        pl.semaphore_signal(barrier, inc=1, device_id=(dp, s, b), device_id_type=MESH)
    for p in (nxt, prv):
        pl.semaphore_signal(barrier, inc=1, device_id=(dp, p, h), device_id_type=MESH)
    pl.semaphore_signal(barrier, inc=1, device_id=(other, s, h), device_id_type=MESH)

    @pl.when(s <= 1)
    def _():
        for k in range(SPANS):
            pltpu.make_async_copy(video.at[0, fr(k)], XP.at[fr(k), pl.ds(1, R)], xpc.at[k]).start()

    @pl.when(s == LAYERS - 1)
    def _():
        for k in range(SPANS):
            pltpu.make_async_copy(ograd.at[0, fr(k)], UR.at[fr(k), pl.ds(1, R)], ur.at[k]).start()

    SS[:, 0:2] = jnp.zeros((2, 2, 6, W16, 3 * C), bf16)
    G[12:14] = jnp.zeros((2, 6, W16, 3 * C), bf16)
    GO[0:1] = gains[...]
    GO[1:2] = shifts[...]
    from_far = (h > 0).astype(jnp.int32) + (h < NB - 1).astype(jnp.int32) + 1
    pl.semaphore_wait(barrier, NB - 1 + 2 + 1 + jnp.where(s == 1, from_far, 0))
    for p in (nxt, prv):
        pl.semaphore_signal(ready, inc=1, device_id=(dp, p, h), device_id_type=MESH)

    @pl.when(s <= 1)
    def _():
        for k in range(SPANS):
            send_edges(video.at[0], 0, 3, XP, k, s_xr.at[k], xph.at[k], s)

    @pl.when(s == LAYERS - 1)
    def _():
        for k in reversed(range(SPANS)):
            send_edges(ograd.at[0], 0, 3, UR, k, s_og.at[k], ur.at[k], s)

    @pl.when(s < LAYERS - 1)
    def _():
        remote(GO, GP, s_gp, gps, (dp, nxt, h))

    @pl.when(s > 0)
    def _():
        await_bytes(GP, gps)

    row = lax.broadcasted_iota(jnp.int32, (1, 6, 1, 1), 1)
    valid = jnp.where(row == 0, (h > 0).astype(f32), jnp.where(row == 5, (h < NB - 1).astype(f32), 1.0))

    def normalized(conv, table_ref, k):
        mu, inv = combine(table_ref[k])
        own = (spread(table_ref[k, h]) - mu).reshape(1, 1, 1, C)
        above = (spread(table_ref[k, up]) - mu).reshape(1, 1, 1, C)
        below = (spread(table_ref[k, dn]) - mu).reshape(1, 1, 1, C)
        off = jnp.concatenate([above, own, own, own, own, below], axis=1)
        return (conv + off) * inv.reshape(1, 1, 1, C)

    gain4 = GO[0:1].reshape(1, 1, 1, C)
    shift4 = GO[1:2].reshape(1, 1, 1, C)

    def layer(k):
        await_bytes(XP.at[fr(k), pl.ds(1, R)], xpc.at[k])

        await_edges(XP, k, xph.at[k])

        @pl.when(s == 0)
        def _():
            x = jnp.where(valid > 0, XP[fr(k)].astype(f32), 0.0)
            XR[fr(k)] = x.astype(bf16)
            put_shifted(SS.at[0], 2 + F * k, x)

        @pl.when(s > 0)
        def _():
            await_bytes(STP.at[k], stp.at[k])
            await_edges(CP, k, cp.at[k], R)
            normed = normalized(CP[fr(k)].astype(f32), STP, k)
            pre = normed * GP[0:1].reshape(1, 1, 1, C) + GP[1:2].reshape(1, 1, 1, C)
            x = XP[fr(k)].astype(f32) + pre * sigmoid(pre)
            x16 = jnp.where(valid > 0, x, 0.0).astype(bf16)
            XR[fr(k)] = x16
            put_shifted(SS.at[0], 2 + F * k, x16.astype(f32))
            NP[k] = normed[:, 1:5].reshape(POS, C)

        @pl.when(k == 0)
        def _():
            wcopy.wait()

        acc = None
        for ab in range(9):
            a, b = divmod(ab, 3)
            lhs = SS[0, fr(k, a), b : b + R].reshape(POS, 3 * C)
            d = jnp.dot(lhs, W[ab * 768 : ab * 768 + 768, :], preferred_element_type=f32)
            acc = d if acc is None else acc + d
        mean = jnp.sum(acc, axis=0, keepdims=True) * (1.0 / POS)
        mean, STO[k, h] = summary(mean, jnp.sum((acc - mean) ** 2, axis=0, keepdims=True))
        cen = acc - mean

        @pl.when((s < LAYERS - 1) & (k == 0))
        def _():
            pl.semaphore_wait(ready, 2)

        @pl.when(s < LAYERS - 1)
        def _():
            for b in bands:
                remote(STO.at[k, h], STP.at[k, h], s_stn.at[k], stp.at[k], (dp, nxt, b))

        for b in bands[:-1]:
            remote(STO.at[k, h], STO.at[k, h], s_sto.at[k], sto.at[k], (dp, s, b))

        CF[fr(k), 1:5] = cen.reshape(F, R, W16, C)
        CO[fr(k)] = cen.astype(bf16).reshape(F, R, W16, C)

        @pl.when(s < LAYERS - 1)
        def _():
            send_edges(CO, 0, 3, CP, k, s_c.at[k], cp.at[k], nxt)
            remote(CO.at[fr(k)], CP.at[fr(k), pl.ds(1, R)], s_c.at[k], cp.at[k], (dp, nxt, h))

        send_edges(CF, 1, 4, CF, k, s_ch.at[k], cfh.at[k], s)
        remote(XR.at[fr(k)], PX.at[fr(k)], s_px.at[k], px.at[k], (other, s, h))

    def own_rows(k):
        await_bytes(STO.at[k, pl.ds(0, NB - 1)], sto.at[k])
        mu, inv = combine(STO[k])
        MI[k] = jnp.concatenate([mu, inv], axis=0)
        off = (spread(STO[k, h]) - mu).reshape(1, 1, 1, C)
        normed = (CF[fr(k), 1:5] + off) * inv.reshape(1, 1, 1, C)
        pre = normed * gain4 + shift4
        sig = sigmoid(pre)
        slope = sig * (1.0 + pre * (1.0 - sig))
        NO[fr(k), 1:5] = normed
        LO[fr(k), 1:5] = slope

        @pl.when(s <= 1)
        def _():
            XN[fr(k)] = (XR[fr(k), 1:5].astype(f32) + pre * sig).astype(bf16)

        @pl.when(s == 0)
        def _():
            remote(XN.at[fr(k)], RL.at[fr(k)], s_x.at[k], rl.at[k], (dp, prv, h))

        @pl.when(s == 1)
        def _():
            far = lax.rem(s + 2, LAYERS)
            send_edges(XN, 0, 3, XP, k, s_xn.at[k], xph.at[k], far)
            remote(XN.at[fr(k)], XP.at[fr(k), pl.ds(1, R)], s_x.at[k], xpc.at[k], (dp, far, h))

        @pl.when(s == LAYERS - 1)
        def _():
            await_edges(UR, k, ur.at[k], R)
            gpre = (UR[fr(k), 1:5].astype(f32) * slope).reshape(POS, C)
            nn = normed.reshape(POS, C)
            SB[k, h] = gradient_summary(gpre, nn, GO[0:1])
            for b in bands[:-1]:
                remote(SB.at[k, h], SB.at[k, h], s_sbo.at[k], sb.at[k], (dp, s, b))

    def own_halo(k):
        await_edges(CF, k, cfh.at[k])
        mu, inv = MI[k, 0:1], MI[k, 1:2]
        for r, b in ((0, up), (5, dn)):
            off = (spread(STO[k, b]) - mu).reshape(1, 1, 1, C)
            normed = (CF[fr(k), r : r + 1] + off) * inv.reshape(1, 1, 1, C)
            pre = normed * gain4 + shift4
            sig = sigmoid(pre)
            NO[fr(k), r : r + 1] = normed
            LO[fr(k), r : r + 1] = sig * (1.0 + pre * (1.0 - sig))

    @pl.when(s == LAYERS - 1)
    def _():
        pl.semaphore_wait(ready, 2)
        for k in range(SPANS):
            await_bytes(RL.at[fr(k)], rl.at[k])
            send_edges(RL, 0, 3, XP, k, s_rl.at[k], xph.at[k], prv)
            remote(RL.at[fr(k)], XP.at[fr(k), pl.ds(1, R)], s_rl.at[k], xpc.at[k], (dp, prv, h))

    def forward(k, carry):
        layer(k)
        return carry

    lax.fori_loop(0, SPANS, forward, 0)

    def own(k, carry):
        own_rows(k)
        return carry

    lax.fori_loop(0, SPANS, own, 0)

    def halo(i, carry):
        own_halo(SPANS - 1 - i)

        @pl.when(s > 0)
        def _():
            pre = NP[i] * GP[0:1] + GP[1:2]
            sig = sigmoid(pre)
            LP[i] = sig * (1.0 + pre * (1.0 - sig))

        return carry

    lax.fori_loop(0, SPANS, halo, 0)

    def partner(k, carry):
        await_bytes(PX.at[fr(k)], px.at[k])
        put_shifted(SS.at[1], 2 + F * k, PX[fr(k)].astype(f32))
        return carry

    lax.fori_loop(0, SPANS, partner, 0)
    WG[...] = jnp.zeros((HALF, C), f32)

    def add_rows(off, rows, lhs, side, k):
        WG[pl.ds(off, rows), :] += lax.dot_general(
            lhs, GG[side, k], (((0,), (0,)), ((), ())), preferred_element_type=f32
        )

    def part(q, side, k):
        ab = q + dp * (8 - 2 * q)
        a, b = lax.div(ab, 3), lax.rem(ab, 3)
        off = pl.multiple_of(ab * 768 - HALF * dp, 128)
        add_rows(off, 768, SS[side, fr(k, a), pl.ds(b, R)].reshape(POS, 3 * C), side, k)

    def middle(side, k):
        off = pl.multiple_of((HALF - 384) * (1 - dp), 128)
        full = SS[side, fr(k, 1), 1 : 1 + R].reshape(POS, 3 * C)
        add_rows(off, 384, jnp.where(dp == 0, full[:, 0:384], full[:, 384:768]), side, k)

    def weight_grad(side, k):
        for q in range(4):
            part(q, side, k)
        middle(side, k)

    TA, TB = 14, 13
    cuts = ((10, 0), (4, 10))

    def tiles(row, n):
        v = WG[pl.ds(pl.multiple_of(row, 8), 8 * n), :].reshape(n, 8, C)
        return jnp.concatenate([v[:, :, 0:128], v[:, :, 128:256]], axis=1)

    def rows(t):
        return jnp.concatenate([t[:, 0:8], t[:, 8:16]], axis=2).reshape(8 * t.shape[0], C)

    def first_phase(m):
        z = m + dp * (3 - 2 * m)
        for y in range(4):
            row = (4 * z + y) * SHARE
            A1S[z, y] = tiles(row, TA).astype(bf16)
            B1S[y, z] = tiles(row + 8 * TA, TB).astype(bf16)
        dz = lax.rem(z - zz + 4, 4)
        n, _ = cuts[0]

        @pl.when(dz != 0)
        def _():
            remote(
                A1S.at[z, :, pl.ds(0, n)], A1R.at[dz - 1, :, pl.ds(0, n)], s_a1.at[0], a1.at[0], (dp, s, 4 * z + yy)
            )

        for dy in range(1, 4):
            y = lax.rem(yy + dy, 4)
            remote(
                B1S.at[y, z, pl.ds(0, n)], B1R.at[dy - 1, z, pl.ds(0, n)], s_b1.at[0], b1.at[0], (dp, s, 4 * zz + y)
            )

    def first_phase_rest():
        n = cuts[0][0]
        for d in range(1, 4):
            z, y = lax.rem(zz + d, 4), lax.rem(yy + d, 4)
            rest = pl.ds(n, TA - n)
            remote(A1S.at[z, :, rest], A1R.at[d - 1, :, rest], s_a1.at[1], a1.at[1], (dp, s, 4 * z + yy))
            rest = pl.ds(n, TB - n)
            remote(B1S.at[y, :, rest], B1R.at[d - 1, :, rest], s_b1.at[1], b1.at[1], (dp, s, 4 * zz + y))

    def backward(i):
        k = SPANS - 1 - i

        @pl.when(s < LAYERS - 1)
        def _():
            await_bytes(SB.at[k], sb.at[k])
            await_edges(UR, k, ur.at[k], R)

        @pl.when(s == LAYERS - 1)
        def _():
            await_bytes(SB.at[k, pl.ds(0, NB - 1)], sb.at[k])

        sums = jnp.sum(SB[k], axis=0)
        gain = GO[0:1]
        means = sums * (1.0 / GSIZE)
        m2, m1 = spread(means), jnp.where(even(means), pltpu.roll(means, C - 1, 1), means)
        upstream = UR[fr(k)].astype(f32)
        gn = upstream * LO[fr(k)] * gain.reshape(1, 1, 1, C)
        nn = NO[fr(k)]
        inv = MI[k, 1:2]
        gc = (gn - m1.reshape(1, 1, 1, C) - nn * m2.reshape(1, 1, 1, C)) * inv.reshape(1, 1, 1, C)
        gc16 = jnp.where(valid > 0, gc, 0.0).astype(bf16)
        GG[0, k] = gc16[:, 1:5].reshape(POS, C)
        remote(GG.at[0, k], GG.at[1, k], s_pg.at[k], pg.at[k], (other, s, h))

        @pl.when(s > 0)
        def _():
            put_shifted(G, F * k, gc16.astype(f32))
            acc = None
            for ab in range(9):
                a, b = divmod(ab, 3)
                for c in range(3):
                    lhs = G[fr(k, a), b : b + R, :, C * c : C * c + C].reshape(POS, C)
                    t = 9 * (2 - a) + 3 * (2 - b) + 2 - c
                    d = lax.dot_general(
                        lhs, W[t * C : t * C + C, :], (((1,), (1,)), ((), ())), preferred_element_type=f32
                    )
                    acc = d if acc is None else acc + d
            u16 = (UR[fr(k), 1:5].astype(f32).reshape(POS, C) + acc).astype(bf16)
            gpre = u16.astype(f32) * LP[k]
            SBO[k] = gradient_summary(gpre, NP[k], GP[0:1])
            for b in bands:
                remote(SBO.at[k], SB.at[k, h], s_sb.at[k], sb.at[k], (dp, prv, b))
            UO[fr(k)] = u16.reshape(F, R, W16, C)
            send_edges(UO, 0, 3, UR, k, s_ur.at[k], ur.at[k], prv)
            remote(UO.at[fr(k)], UR.at[fr(k), pl.ds(1, R)], s_ur.at[k], ur.at[k], (dp, prv, h))

        @pl.when((s == 0) & ((dp == 1) | (k > 0)))
        def _():
            weight_grad(0, k)

        if i == 0:

            @pl.when((s == 0) & (dp == 0))
            def _():
                await_bytes(GG.at[1, 0], pg.at[0])
                weight_grad(1, 0)

    @pl.when((s == 0) & (dp == 0))
    def _():
        def term(i, carry):
            k = SPANS - 1 - i
            await_bytes(GG.at[1, k], pg.at[k])
            weight_grad(1, k)
            return carry

        lax.fori_loop(0, SPANS - 1, term, 0)

    for i in range(SPANS):
        backward(i)

    @pl.when((s > 0) | (dp == 1))
    def _():
        await_bytes(GG.at[1, 2], pg.at[2])
        await_bytes(GG.at[1, 1], pg.at[1])

    @pl.when((s > 0) & (dp == 0))
    def _():
        await_bytes(GG.at[1, 0], pg.at[0])

    def term(t, carry):
        late = (t >= 2 + dp).astype(jnp.int32)
        weight_grad(late, SPANS - 1 - (t - late * (2 + dp)))
        return carry

    lax.fori_loop(jnp.where(s > 0, 0, jnp.where(dp == 1, 3, 5)), 5, term, 0)

    @pl.when(dp == 1)
    def _():
        await_bytes(GG.at[1, 0], pg.at[0])

    for q in range(4):
        part(q, dp, 0)
        if q > 0:
            first_phase(q - 1)
    middle(dp, 0)
    first_phase(3)
    first_phase_rest()

    def norm_terms(k, total):
        gpre = (UR[fr(k), 1:5].astype(f32) * LO[fr(k), 1:5]).reshape(POS, C)
        both = jnp.concatenate(
            [
                jnp.sum(gpre * NO[fr(k), 1:5].reshape(POS, C), axis=0, keepdims=True),
                jnp.sum(gpre, axis=0, keepdims=True),
            ],
            axis=0,
        )
        return total + both

    NT[h] = lax.fori_loop(0, SPANS, norm_terms, jnp.zeros((2, C), f32))
    for b in bands[:-1]:
        remote(NT.at[h], NT.at[h], s_nt, nt, (dp, s, b))

    def total(r, *at):
        return sum(r[(j, *at)].astype(f32) for j in range(3))

    for i, (n, t0) in enumerate(cuts):
        span = pl.ds(t0, n)
        await_bytes(A1R.at[:, :, span], a1.at[i])
        for dy in range(1, 4):
            y = lax.rem(yy + dy, 4)
            A2S[dy - 1, span] = (tiles((4 * zz + y) * SHARE + 8 * t0, n) + total(A1R, y, span)).astype(bf16)
            remote(A2S.at[dy - 1, span], A2R.at[dy - 1, span], s_a2, a2, (dp, s, 4 * zz + y))
        n = min(n, TB - t0)
        span = pl.ds(t0, n)
        await_bytes(B1R.at[:, :, span], b1.at[i])
        for dz in range(1, 4):
            z = lax.rem(zz + dz, 4)
            row = (4 * z + yy) * SHARE + 8 * (TA + t0)
            B2S[dz - 1, span] = (tiles(row, n) + total(B1R, z, span)).astype(bf16)
            remote(B2S.at[dz - 1, span], B2R.at[dz - 1, span], s_b2, b2, (dp, s, 4 * z + yy))
    await_bytes(NT.at[pl.ds(0, NB - 1)], nt)
    NG[0] = jnp.sum(NT[...], axis=0)
    remote(NG.at[0], NG.at[1], s_ng, ngs, (other, s, h))
    mine_a = tiles(h * SHARE, TA) + total(A1R, yy)
    mine_b = tiles(h * SHARE + 8 * TA, TB) + total(B1R, zz)
    await_bytes(A2R, a2)
    out_k[0, 0 : 8 * TA] = rows(mine_a + total(A2R))
    await_bytes(B2R, b2)
    out_k[0, 8 * TA : SHARE] = rows(mine_b + total(B2R))
    await_bytes(NG.at[1], ngs)
    out_n[0] = NG[0] + NG[1]

    for k in range(SPANS):
        await_bytes(STO.at[k, pl.ds(0, NB - 1)], s_sto.at[k])
        await_edges(CF, k, s_ch.at[k])
        await_bytes(PX.at[fr(k)], s_px.at[k])
        await_bytes(GG.at[0, k], s_pg.at[k])

        @pl.when(s < LAYERS - 1)
        def _():
            await_bytes(STP.at[k], s_stn.at[k])
            await_edges(CP, k, s_c.at[k], R)

        @pl.when(s <= 1)
        def _():
            await_bytes(XN.at[fr(k)], s_x.at[k])

            await_edges(XP, k, s_xr.at[k])

        @pl.when(s == 1)
        def _():
            await_edges(XP, k, s_xn.at[k])

        @pl.when(s > 0)
        def _():
            await_edges(UR, k, s_ur.at[k], R)
            await_bytes(SB.at[k], s_sb.at[k])

        @pl.when(s == LAYERS - 1)
        def _():
            await_edges(XP, k, s_rl.at[k], R)
            await_edges(UR, k, s_og.at[k])
            await_bytes(SB.at[k, pl.ds(0, NB - 1)], s_sbo.at[k])

    @pl.when(s < LAYERS - 1)
    def _():
        await_bytes(GO, s_gp)

    await_bytes(NG.at[0], s_ng)
    await_bytes(NT.at[pl.ds(0, NB - 1)], s_nt)
    for i, (n, t0) in enumerate(cuts):
        await_bytes(A1R.at[:, :, pl.ds(t0, n)], s_a1.at[i])
        await_bytes(B1R.at[:, :, pl.ds(t0, min(n, TB - t0))], s_b1.at[i])
    await_bytes(A2R, s_a2)
    await_bytes(B2R, s_b2)


def per_device(video, kernels, gains, shifts, out_grad):
    dma = pltpu.SemaphoreType.DMA
    six = (F * SPANS, 6, W16, C)
    four = (F * SPANS, R, W16, C)
    wide = (F * SPANS + 2, 6, W16, 3 * C)
    scratch = [
        pltpu.VMEM((27 * C, C), bf16),
        pltpu.VMEM(six, bf16),
        pltpu.VMEM(six, bf16),
        pltpu.VMEM(four, bf16),
        pltpu.VMEM(four, bf16),
        pltpu.VMEM(six, bf16),
        pltpu.VMEM(four, bf16),
        pltpu.VMEM(six, f32),
        pltpu.VMEM((2,) + wide, bf16),
        pltpu.VMEM(six, bf16),
        pltpu.VMEM(wide, bf16),
        pltpu.VMEM((2, SPANS, POS, C), bf16),
        pltpu.VMEM(six, bf16),
        pltpu.VMEM(four, bf16),
        pltpu.VMEM((SPANS, NB, 1, C), f32),
        pltpu.VMEM((SPANS, NB, 1, C), f32),
        pltpu.VMEM((SPANS, NB, 1, C), f32),
        pltpu.VMEM((SPANS, 1, C), f32),
        pltpu.VMEM((2, C), f32),
        pltpu.VMEM((2, C), f32),
        pltpu.VMEM((SPANS, POS, C), f32),
        pltpu.VMEM((SPANS, POS, C), f32),
        pltpu.VMEM(six, f32),
        pltpu.VMEM(six, f32),
        pltpu.VMEM((SPANS, 2, C), f32),
        pltpu.VMEM((HALF, C), f32),
        pltpu.VMEM((4, 4, 14, 16, 128), bf16),
        pltpu.VMEM((3, 4, 14, 16, 128), bf16),
        pltpu.VMEM((4, 4, 13, 16, 128), bf16),
        pltpu.VMEM((3, 4, 13, 16, 128), bf16),
        pltpu.VMEM((3, 14, 16, 128), bf16),
        pltpu.VMEM((3, 14, 16, 128), bf16),
        pltpu.VMEM((3, 13, 16, 128), bf16),
        pltpu.VMEM((3, 13, 16, 128), bf16),
        pltpu.VMEM((2, 2, C), f32),
        pltpu.VMEM((NB, 2, C), f32),
    ]
    k3 = dma((SPANS,))
    two = dma((2,))
    sems = [pltpu.SemaphoreType.REGULAR, dma] + [k3] * 11 + [two, two] + [dma] * 5
    sems += [k3] * 14 + [two, two] + [dma] * 5
    anyspec = pl.BlockSpec(memory_space=pl.ANY)
    vm = pl.BlockSpec(memory_space=pltpu.VMEM)
    return pl.pallas_call(
        kernel,
        out_shape=(
            pltpu.VMEM((1, SHARE, C), f32),
            pltpu.VMEM((1, 2, C), f32),
        ),
        in_specs=[anyspec, anyspec, vm, vm, anyspec],
        out_specs=(vm, vm),
        scratch_shapes=scratch + sems,
        compiler_params=pltpu.CompilerParams(
            collective_id=0, has_side_effects=True, vmem_limit_bytes=60 * 2**20
        ),
    )(video, kernels, gains, shifts, out_grad)


def solution(mesh):
    return jax.shard_map(
        per_device,
        mesh=mesh,
        in_specs=(
            P("dp", None, "height", None, None),
            P("pipe", None, None),
            P("pipe", None),
            P("pipe", None),
            P("dp", None, "height", None, None),
        ),
        out_specs=(P("pipe", ("dp", "height"), None), P("pipe", None, None)),
        check_vma=False,
    )
```

profile of v0, /device:TPU:1, one launch (start us, length us, event | category | flops | bytes accessed | tf_op | source)
XLA Modules:
  0.0 107.3 jit_solution(5877196077229965097)
XLA Ops:
  0.6 105.4 %shard_map.68 = (f32[1,216,256]{2,1,0:T(8,128)S(1)}, f32[1,2,256]{2,1,0:T(2,128)S(1)}) custom-call(bf16[1,12,4,16,256]{4,3,2,1,0:T(8,128)(2,1)} %video.1, bf16[1,6912,256]{2,1,0:T(8,128)(2,1)} %kern.1, f32[1,256]{1,0:T(1,128)} %gains.1, f32[1,256]{1,0:T(1,128)} %shifts.1, bf16[1,12,4,16,256]{4,3,2,1,0:T(8,128)(2,1)} %ograd.1), custom_call_target="tpu_custom_call" | custom-call | tf_op jit(solution)/shard_map/pallas_call | solution.py:658
  106.0 0.7 copy.9
  106.7 0.6 copy.10
where the time goes:
time: 108 us; the launch traced here: 107 us
  Pallas kernels  105 us (97%)
  local copies, waits for them, and re-layouts  1.27 us (1%)
    pallas_call x1, Pallas kernels, per_device(): pl.pallas_call(kernel, out_shape=(pltpu.VMEM((1, SHARE, C), f32), pltpu.V...  105 us

commit v1 on v0

--- a/solution.py
+++ b/solution.py
@@ -378,7 +378,7 @@
         middle(side, k)
 
     TA, TB = 14, 13
-    cuts = ((10, 0), (4, 10))
+    cuts = ((12, 0), (2, 12))
 
     def tiles(row, n):
         v = WG[pl.ds(pl.multiple_of(row, 8), 8 * n), :].reshape(n, 8, C)

time: 108 us -> 107 us (level)
  no operation moved by 1% of the time
where the time goes in v1:
time: 107 us
  Pallas kernels  105 us (98%)
  local copies, waits for them, and re-layouts  1.27 us (1%)
    pallas_call x1, Pallas kernels, per_device(): pl.pallas_call(kernel, out_shape=(pltpu.VMEM((1, SHARE, C), f32), pltpu.V...  105 us

profile of v1, /device:TPU:1, one launch (start us, length us, event | category | flops | bytes accessed | tf_op | source)
XLA Modules:
  0.0 106.9 jit_solution(17988923083370228495)
XLA Ops:
  0.6 105.0 %shard_map.68 = (f32[1,216,256]{2,1,0:T(8,128)S(1)}, f32[1,2,256]{2,1,0:T(2,128)S(1)}) custom-call(bf16[1,12,4,16,256]{4,3,2,1,0:T(8,128)(2,1)} %video.1, bf16[1,6912,256]{2,1,0:T(8,128)(2,1)} %kern.1, f32[1,256]{1,0:T(1,128)} %gains.1, f32[1,256]{1,0:T(1,128)} %shifts.1, bf16[1,12,4,16,256]{4,3,2,1,0:T(8,128)(2,1)} %ograd.1), custom_call_target="tpu_custom_call" | custom-call | tf_op jit(solution)/shard_map/pallas_call | solution.py:658
  105.6 0.7 copy.9
  106.3 0.6 copy.10

commit v2 on v1

--- a/solution.py
+++ b/solution.py
@@ -423,7 +423,14 @@
         @pl.when(s < LAYERS - 1)
         def _():
             await_bytes(SB.at[k], sb.at[k])
+
+        @pl.when((s > 0) & (s < LAYERS - 1))
+        def _():
             await_edges(UR, k, ur.at[k], R)
+
+        @pl.when(s == 0)
+        def _():
+            await_bytes(UR.at[fr(k), pl.ds(1, R)], ur.at[k])
 
         @pl.when(s == LAYERS - 1)
         def _():
@@ -461,7 +468,11 @@
             for b in bands:
                 remote(SBO.at[k], SB.at[k, h], s_sb.at[k], sb.at[k], (dp, prv, b))
             UO[fr(k)] = u16.reshape(F, R, W16, C)
-            send_edges(UO, 0, 3, UR, k, s_ur.at[k], ur.at[k], prv)
+
+            @pl.when(s > 1)
+            def _():
+                send_edges(UO, 0, 3, UR, k, s_ur.at[k], ur.at[k], prv)
+
             remote(UO.at[fr(k)], UR.at[fr(k), pl.ds(1, R)], s_ur.at[k], ur.at[k], (dp, prv, h))
 
         @pl.when((s == 0) & ((dp == 1) | (k > 0)))
@@ -584,8 +595,15 @@
 
         @pl.when(s > 0)
         def _():
+            await_bytes(SB.at[k], s_sb.at[k])
+
+        @pl.when(s > 1)
+        def _():
             await_edges(UR, k, s_ur.at[k], R)
-            await_bytes(SB.at[k], s_sb.at[k])
+
+        @pl.when(s == 1)
+        def _():
+            await_bytes(UR.at[fr(k), pl.ds(1, R)], s_ur.at[k])
 
         @pl.when(s == LAYERS - 1)
         def _():

time: 107 us -> 106 us (level)
    pallas_call x1, Pallas kernels: 105 us -> 104 us  [per_device(): pl.pallas_call(kernel, out_shape=(pltpu.VMEM((1, SHARE, C), f32), pltpu.V...]
where the time goes in v2:
time: 106 us
  Pallas kernels  104 us (98%)
  local copies, waits for them, and re-layouts  1.27 us (1%)
    pallas_call x1, Pallas kernels, per_device(): pl.pallas_call(kernel, out_shape=(pltpu.VMEM((1, SHARE, C), f32), pltpu.V...  104 us

profile of v2, /device:TPU:1, one launch (start us, length us, event | category | flops | bytes accessed | tf_op | source)
XLA Modules:
  0.0 105.8 jit_solution(17634072656345578938)
XLA Ops:
  0.6 103.9 %shard_map.68 = (f32[1,216,256]{2,1,0:T(8,128)S(1)}, f32[1,2,256]{2,1,0:T(2,128)S(1)}) custom-call(bf16[1,12,4,16,256]{4,3,2,1,0:T(8,128)(2,1)} %video.1, bf16[1,6912,256]{2,1,0:T(8,128)(2,1)} %kern.1, f32[1,256]{1,0:T(1,128)} %gains.1, f32[1,256]{1,0:T(1,128)} %shifts.1, bf16[1,12,4,16,256]{4,3,2,1,0:T(8,128)(2,1)} %ograd.1), custom_call_target="tpu_custom_call" | custom-call | tf_op jit(solution)/shard_map/pallas_call | solution.py:676
  104.5 0.7 copy.9
  105.2 0.6 copy.10

commit v3 on v2

--- a/solution.py
+++ b/solution.py
@@ -447,7 +447,10 @@
         gc = (gn - m1.reshape(1, 1, 1, C) - nn * m2.reshape(1, 1, 1, C)) * inv.reshape(1, 1, 1, C)
         gc16 = jnp.where(valid > 0, gc, 0.0).astype(bf16)
         GG[0, k] = gc16[:, 1:5].reshape(POS, C)
-        remote(GG.at[0, k], GG.at[1, k], s_pg.at[k], pg.at[k], (other, s, h))
+
+        @pl.when(s == 0)
+        def _():
+            remote(GG.at[0, k], GG.at[1, k], s_pg.at[k], pg.at[k], (other, s, h))
 
         @pl.when(s > 0)
         def _():
@@ -474,6 +477,7 @@
                 send_edges(UO, 0, 3, UR, k, s_ur.at[k], ur.at[k], prv)
 
             remote(UO.at[fr(k)], UR.at[fr(k), pl.ds(1, R)], s_ur.at[k], ur.at[k], (dp, prv, h))
+            remote(GG.at[0, k], GG.at[1, k], s_pg.at[k], pg.at[k], (other, s, h))
 
         @pl.when((s == 0) & ((dp == 1) | (k > 0)))
         def _():

time: 106 us -> 106 us (level)
  no operation moved by 1% of the time
where the time goes in v3:
time: 106 us
  Pallas kernels  104 us (98%)
  local copies, waits for them, and re-layouts  1.27 us (1%)
    pallas_call x1, Pallas kernels, per_device(): pl.pallas_call(kernel, out_shape=(pltpu.VMEM((1, SHARE, C), f32), pltpu.V...  104 us

profile of v3, /device:TPU:1, one launch (start us, length us, event | category | flops | bytes accessed | tf_op | source)
XLA Modules:
  0.0 105.8 jit_solution(11181142070571993313)
XLA Ops:
  0.6 103.9 %shard_map.68 = (f32[1,216,256]{2,1,0:T(8,128)S(1)}, f32[1,2,256]{2,1,0:T(2,128)S(1)}) custom-call(bf16[1,12,4,16,256]{4,3,2,1,0:T(8,128)(2,1)} %video.1, bf16[1,6912,256]{2,1,0:T(8,128)(2,1)} %kern.1, f32[1,256]{1,0:T(1,128)} %gains.1, f32[1,256]{1,0:T(1,128)} %shifts.1, bf16[1,12,4,16,256]{4,3,2,1,0:T(8,128)(2,1)} %ograd.1), custom_call_target="tpu_custom_call" | custom-call | tf_op jit(solution)/shard_map/pallas_call | solution.py:680
  104.5 0.7 copy.9
  105.2 0.6 copy.10
